TPU v7x, 1024 devices: a whole 4x4x32 slice. The times are simulated.
1024 devices in a mesh: node: 64 (over z, core), local: 16 (over x, y).
Axes of the slice: x: 4, y: 4, z: 32, core: 2. Of those that a mesh axis runs over, the one named last changes fastest.
Arguments:
- hidden_in: bfloat16 [4096, 7168], P('node', 'local'), may hold values from -6 to 6
- expert_ids: int32 [4096, 4], P('node'), may hold values from 0 to 63, all different within a row; in each aligned block of 64 rows (0 to 63, 64 to 127, ...) at most 8 rows name the same one
- gate_weights: float32 [4096, 4], P('node'), may hold values from 0.1 to 0.9
- w_in: bfloat16 [64, 7168, 2048], P('node', None, 'local'), may hold values from -0.0625 to 0.0625
- w_down: bfloat16 [64, 1024, 7168], P('node', None, 'local'), may hold values from -0.1875 to 0.1875
Outputs:
- mixed: bfloat16 [4096, 7168], P('node', 'local')
Inputs may be any that keep to these rules, and one draw needn't show every extreme that they name: `expert_ids`: each token names 4 different experts. Among the tokens of one node group no expert is named more than 8 times, and in every draw some expert is named exactly 8 times by some group.
All inputs are finite; a program needn't handle non-finite values.
Results may differ from a plain program's by a relative error of at most 0.0057.
Values may be sent and summed in bfloat16 or wider, within the bound.
No kernel may reach another device: no remote copies, remote signals or barrier semaphores. Data moves between devices by JAX's collectives and lax.ppermute only.
A program may use at most 64 MiB of HBM per device.

v0:
```python
import jax
import jax.numpy as jnp
from jax import lax
from jax.sharding import Mesh, PartitionSpec as P

FAR = 4
MID = 4
NODES = ("far", "mid", "near")


def split_float(values):
    high = lax.reduce_precision(values, 8, 7)
    rest = values - high
    middle = lax.reduce_precision(rest, 8, 7)
    return [high, middle, rest - middle]


def route_masks(ids, first, experts, capacity):
    tok_count, top_count = ids.shape[-2:]
    lane = jnp.arange(experts * capacity, dtype=jnp.int32)
    expert = first + lane // capacity
    named = [ids[..., k, None] == expert for k in range(top_count)]
    chosen = named[0]
    for hit in named[1:]:
        chosen = chosen | hit
    order = jnp.arange(tok_count, dtype=jnp.int32)
    before = (order[None, :] < order[:, None]).astype(jnp.bfloat16)
    slot = jnp.einsum(
        "tu,...uj->...tj", before, chosen.astype(jnp.bfloat16), preferred_element_type=jnp.float32
    )
    placed = chosen & (slot == (lane % capacity).astype(jnp.float32))
    return named, placed


def swap(blocks, axis):
    return lax.all_to_all(blocks, axis, split_axis=0, concat_axis=0, tiled=True)


def spread(block, axis):
    size = lax.axis_size(axis)
    return swap(jnp.broadcast_to(block[None], (size, *block.shape)), axis)


def local(hidden_in, expert_ids, gate_weights, w_in, w_down):
    far, mid, near = (lax.axis_size(axis) for axis in NODES)
    parts = lax.axis_size("local")
    tok_count, features = hidden_in.shape
    top_count = expert_ids.shape[1]
    nodes = far * mid * near
    capacity = max(2, (2 * tok_count * top_count + nodes - 1) // nodes)
    rows = nodes * capacity
    columns = w_in.shape[2]
    block = lax.axis_index("far") * mid + lax.axis_index("mid")

    weights = swap(w_in.reshape(parts, features, columns), "local")

    routing = [expert_ids.astype(jnp.float32)] + split_float(gate_weights)
    routing = jnp.concatenate(routing, axis=1).astype(jnp.bfloat16)
    payload = jnp.concatenate([hidden_in, routing], axis=1)
    gathered = lax.all_gather(payload, ("far", "mid"), axis=0)
    gathered = jnp.roll(gathered, -lax.axis_index("far") * mid, axis=0)
    routing = gathered[:, :, features:]
    ids = routing[:, :, :top_count].astype(jnp.int32)

    _, placed = route_masks(ids, block * near, near, capacity)
    outgoing = jnp.einsum(
        "gtj,gtd->gjd",
        placed.astype(jnp.bfloat16),
        gathered[:, :, :features],
        preferred_element_type=jnp.float32,
    ).astype(jnp.bfloat16)
    outgoing = outgoing.reshape(far * mid, near, capacity, features).transpose(1, 0, 2, 3)
    outgoing, weights = lax.optimization_barrier((outgoing, weights))
    arrived = swap(outgoing, "near").reshape(near, far, mid, capacity, features)
    arrived = arrived.transpose(2, 0, 1, 3, 4).reshape(rows, features)

    partial = jnp.einsum(
        "rd,ldj->lrj", arrived, weights, preferred_element_type=jnp.float32
    ).astype(jnp.bfloat16)
    projected = jnp.sum(swap(partial, "local").astype(jnp.float32), axis=0)
    gate_part = projected[:, : columns // 2]
    up_part = projected[:, columns // 2 :]
    activated = (jax.nn.silu(gate_part) * up_part).astype(jnp.bfloat16)
    activated = spread(activated.T, "local").reshape(-1, rows)

    expert_out = lax.dot_general(
        activated, w_down[0], (((0,), (0,)), ((), ())), preferred_element_type=jnp.float32
    ).astype(jnp.bfloat16)
    expert_out = expert_out.reshape(mid * near, far, capacity, features)

    routing = routing.reshape(far, mid, tok_count, -1)
    routing = lax.dynamic_index_in_dim(routing, lax.axis_index("mid"), 1, keepdims=False)
    ids = routing[:, :, :top_count].astype(jnp.int32)
    named, placed = route_masks(ids, lax.axis_index("far") * mid * near, mid * near, capacity)
    combine = []
    for piece in (1, 2, 3):
        gates = routing[:, :, piece * top_count : (piece + 1) * top_count]
        combine.append(
            sum(jnp.where(hit & placed, gates[:, :, k, None], 0) for k, hit in enumerate(named))
        )

    returned = swap(expert_out, ("mid", "near")).transpose(1, 0, 2, 3)
    returned = returned.reshape(far, mid * near * capacity, features)

    def block_sums(first, last):
        return sum(
            jnp.einsum(
                "gtj,gjd->gtd",
                piece[first:last],
                returned[first:last],
                preferred_element_type=jnp.float32,
            )
            for piece in combine
        )

    away = block_sums(1, far).astype(jnp.bfloat16)
    sent = [
        lax.ppermute(away[step - 1], "far", [(i, (i + step) % far) for i in range(far)])
        for step in sorted(range(1, far), key=lambda step: -min(step, far - step))
    ]
    mixed = block_sums(0, 1)[0]
    for block in sent:
        mixed += block.astype(jnp.float32)
    return mixed.astype(jnp.bfloat16)


def solution(mesh):
    node, parts = mesh.devices.shape
    split = mesh.devices.reshape(FAR, MID, node // (FAR * MID), parts)
    split = Mesh(split, (*NODES, "local"))
    in_specs = (
        P(NODES, "local"),
        P(NODES, None),
        P(NODES, None),
        P(NODES, None, "local"),
        P(NODES, None, "local"),
    )
    out_specs = P(NODES, "local")
    return jax.shard_map(
        local, mesh=split, in_specs=in_specs, out_specs=out_specs, check_vma=False
    )
```

profile of v0, /device:TPU:6, one launch (start us, length us, event | category | flops | bytes accessed | tf_op | source)
XLA Modules:
  0.0 213.3 jit_solution(3941124605899609820)
XLA Ops:
  0.0 17.5 %all-to-all-start = ((bf16[16,448,128]{2,1,0:T(8,128)(2,1)}), bf16[16,448,128]{2,1,0:T(8,128)(2,1)}, u32[]{:S(2)}, u32[]{:S(2)}) async-start(bf16[16,448,128]{2,1,0:T(8,128)(2,1)} %bitcast.109), calls=%async_computation | async-start | bytes 3670016 | tf_op jit(solution)/shard_map/all_to_all | solution.py:36
  18.1 47.6 %all-gather = bf16[1024,464]{1,0:T(8,128)(2,1)S(1)} all-gather(bf16[64,464]{1,0:T(8,128)(2,1)S(1)} %concatenate.10), channel_id=2, replica_groups=mesh['far'=4,'mid'=4,'near'=4,'local'=16] {'far','mid'}, dimensions={0}, use_global_device_ids=true | all-gather | bytes 1009664 | tf_op jit(solution)/shard_map/all_gather | solution.py:60
  65.7 0.4 fusion.6
  66.3 1.6 slice_reduce_fusion.3
  67.9 0.5 fusion
  68.5 11.2 %all_to_all.25 = bf16[4,16,8,448]{3,2,1,0:T(8,128)(2,1)S(1)} all-to-all(bf16[4,16,8,448]{3,2,1,0:T(8,128)(2,1)S(1)} %bitcast.107), channel_id=1, replica_groups=mesh['far'=4,'mid'=4,'near'=4,'local'=16] {'near'}, dimensions={0} | all-to-all | bytes 917504 | tf_op jit(solution)/shard_map/all_to_all | solution.py:36
  79.8 2.8 %convert_bitcast_fusion = bf16[16,512,128]{1,2,0:T(8,128)(2,1)S(1)} fusion(bf16[16,448,128]{2,1,0:T(8,128)(2,1)} %all-to-all-done, bf16[512,448,1]{1,0,2:T(8,128)(2,1)S(1)} %bitcast.117), kind=kOutput, calls=%fused_computation.3 | convolution fusion | flops 940572672 | bytes 4390912 | tf_op jit(solution)/shard_map/rd,ldj->lrj/dot_general | solution.py:77
  82.6 34.6 %all_to_all.26 = bf16[16,512,128]{1,2,0:T(8,128)(2,1)S(1)} all-to-all(bf16[16,512,128]{1,2,0:T(8,128)(2,1)S(1)} %convert_bitcast_fusion), channel_id=1, replica_groups=mesh['far'=4,'mid'=4,'near'=4,'local'=16] {'local'}, dimensions={0} | all-to-all | bytes 4194304 | tf_op jit(solution)/shard_map/all_to_all | solution.py:36
  117.3 0.3 convert_reduce_fusion
  117.7 19.1 %all_to_all.27 = bf16[16,64,512]{2,1,0:T(8,128)(2,1)S(1)} all-to-all(bf16[16,64,512]{2,1,0:T(8,128)(2,1)S(1)} %broadcast_in_dim.131), channel_id=1, replica_groups=mesh['far'=4,'mid'=4,'near'=4,'local'=16] {'local'}, dimensions={0} | all-to-all | bytes 2097152 | tf_op jit(solution)/shard_map/all_to_all | solution.py:36
  136.8 0.6 convolution_convert_fusion.1
  137.5 1.0 copy.48
  138.5 3.9 %all-to-all-start.4 = ((bf16[16,4,8,448]{3,2,1,0:T(8,128)(2,1)}), bf16[16,4,8,448]{3,2,1,0:T(8,128)(2,1)S(1)}, u32[]{:S(2)}, u32[]{:S(2)}) async-start(bf16[16,4,8,448]{3,2,1,0:T(8,128)(2,1)} %bitcast.26), calls=%async_computation.4 | async-start | bytes 1048576 | tf_op jit(solution)/shard_map/all_to_all | solution.py:36
  142.7 0.9 select_add_fusion
  143.6 24.6 %all-to-all-done.4 = bf16[16,4,8,448]{3,2,1,0:T(8,128)(2,1)S(1)} async-done(((bf16[16,4,8,448]{3,2,1,0:T(8,128)(2,1)}), bf16[16,4,8,448]{3,2,1,0:T(8,128)(2,1)S(1)}, u32[]{:S(2)}, u32[]{:S(2)}) %all-to-all-start.4) | async-done | bytes 458784 | tf_op jit(solution)/shard_map/all_to_all | solution.py:36
  168.3 0.4 fusion.11
  168.8 0.4 convolution_add_fusion.1
  169.2 0.4 fusion.1
  169.6 14.9 %collective-permute-start = (bf16[64,448]{1,0:T(8,128)(2,1)S(1)}, bf16[64,448]{1,0:T(8,128)(2,1)S(1)}, u32[]{:S(2)}, u32[]{:S(2)}) collective-permute-start(bf16[64,448]{1,0:T(8,128)(2,1)S(1)} %get-tuple-element.13), channel_id=1, source_target_pairs={{0,512},{256,768},{512,0},{768,256},{1,513},{257,769},{513,1},{769... | collective-permute-start | bytes 172040 | tf_op jit(solution)/shard_map/ppermute | solution.py:118
  184.5 6.3 %collective-permute-start.2 = (bf16[64,448]{1,0:T(8,128)(2,1)S(1)}, bf16[64,448]{1,0:T(8,128)(2,1)S(1)}, u32[]{:S(2)}, u32[]{:S(2)}) collective-permute-start(bf16[64,448]{1,0:T(8,128)(2,1)S(1)} %get-tuple-element.14), channel_id=1, source_target_pairs={{0,768},{256,0},{512,256},{768,512},{1,769},{257,1},{513,257},{769... | collective-permute-start | bytes 172040 | tf_op jit(solution)/shard_map/ppermute | solution.py:118
  190.8 8.3 %collective-permute-start.1 = (bf16[64,448]{1,0:T(8,128)(2,1)S(1)}, bf16[64,448]{1,0:T(8,128)(2,1)S(1)}, u32[]{:S(2)}, u32[]{:S(2)}) collective-permute-start(bf16[64,448]{1,0:T(8,128)(2,1)S(1)} %get-tuple-element.15), channel_id=1, source_target_pairs={{0,256},{256,512},{512,768},{768,0},{1,257},{257,513},{513,769},{7... | collective-permute-start | bytes 172040 | tf_op jit(solution)/shard_map/ppermute | solution.py:118
  199.2 12.9 %collective-permute-done.2 = bf16[64,448]{1,0:T(8,128)(2,1)S(1)} collective-permute-done((bf16[64,448]{1,0:T(8,128)(2,1)S(1)}, bf16[64,448]{1,0:T(8,128)(2,1)S(1)}, u32[]{:S(2)}, u32[]{:S(2)}) %collective-permute-start.2) | collective-permute-done | bytes 57376 | tf_op jit(solution)/shard_map/ppermute | solution.py:118
  212.1 0.4 collective-permute-done.1
  212.5 0.8 add_convert_fusion
  (34 shorter events, 1.6 us)
Async XLA Ops:
  0.0 136.8 %copy-start = (bf16[1,1024,448]{1,2,0:T(8,128)(2,1)S(1)}, bf16[1,1024,448]{1,2,0:T(8,128)(2,1)}, u32[]{:S(2)}) copy-start(bf16[1,1024,448]{1,2,0:T(8,128)(2,1)} %param.9) | copy-start | bytes 2752516
  0.0 17.5 %copy-start.3 = (f32[64,4]{0,1:T(4,128)S(1)}, f32[64,4]{0,1:T(4,128)}, u32[]{:S(2)}) copy-start(f32[64,4]{0,1:T(4,128)} %param.7) | copy-start | bytes 3076
  0.0 17.6 %copy-start.2 = (s32[64,4]{0,1:T(4,128)S(1)}, s32[64,4]{0,1:T(4,128)}, u32[]{:S(2)}) copy-start(s32[64,4]{0,1:T(4,128)} %param.6) | copy-start | bytes 3076
  0.0 18.0 %copy-start.1 = (bf16[64,448]{1,0:T(8,128)(2,1)S(1)}, bf16[64,448]{1,0:T(8,128)(2,1)}, u32[]{:S(2)}) copy-start(bf16[64,448]{1,0:T(8,128)(2,1)} %param.5) | copy-start | bytes 172036
  0.0 68.4 %all-to-all-start = ((bf16[16,448,128]{2,1,0:T(8,128)(2,1)}), bf16[16,448,128]{2,1,0:T(8,128)(2,1)}, u32[]{:S(2)}, u32[]{:S(2)}) async-start(bf16[16,448,128]{2,1,0:T(8,128)(2,1)} %bitcast.109), calls=%async_computation | async-start | bytes 3670016 | tf_op jit(solution)/shard_map/all_to_all | solution.py:36
  138.5 29.7 %all-to-all-start.4 = ((bf16[16,4,8,448]{3,2,1,0:T(8,128)(2,1)}), bf16[16,4,8,448]{3,2,1,0:T(8,128)(2,1)S(1)}, u32[]{:S(2)}, u32[]{:S(2)}) async-start(bf16[16,4,8,448]{3,2,1,0:T(8,128)(2,1)} %bitcast.26), calls=%async_computation.4 | async-start | bytes 1048576 | tf_op jit(solution)/shard_map/all_to_all | solution.py:36
  169.6 29.6 %collective-permute-start = (bf16[64,448]{1,0:T(8,128)(2,1)S(1)}, bf16[64,448]{1,0:T(8,128)(2,1)S(1)}, u32[]{:S(2)}, u32[]{:S(2)}) collective-permute-start(bf16[64,448]{1,0:T(8,128)(2,1)S(1)} %get-tuple-element.13), channel_id=1, source_target_pairs={{0,512},{256,768},{512,0},{768,256},{1,513},{257,769},{513,1},{769... | collective-permute-start | bytes 172040 | tf_op jit(solution)/shard_map/ppermute | solution.py:118
  184.5 27.6 %collective-permute-start.2 = (bf16[64,448]{1,0:T(8,128)(2,1)S(1)}, bf16[64,448]{1,0:T(8,128)(2,1)S(1)}, u32[]{:S(2)}, u32[]{:S(2)}) collective-permute-start(bf16[64,448]{1,0:T(8,128)(2,1)S(1)} %get-tuple-element.14), channel_id=1, source_target_pairs={{0,768},{256,0},{512,256},{768,512},{1,769},{257,1},{513,257},{769... | collective-permute-start | bytes 172040 | tf_op jit(solution)/shard_map/ppermute | solution.py:118
  190.8 21.7 %collective-permute-start.1 = (bf16[64,448]{1,0:T(8,128)(2,1)S(1)}, bf16[64,448]{1,0:T(8,128)(2,1)S(1)}, u32[]{:S(2)}, u32[]{:S(2)}) collective-permute-start(bf16[64,448]{1,0:T(8,128)(2,1)S(1)} %get-tuple-element.15), channel_id=1, source_target_pairs={{0,256},{256,512},{512,768},{768,0},{1,257},{257,513},{513,769},{7... | collective-permute-start | bytes 172040 | tf_op jit(solution)/shard_map/ppermute | solution.py:118
where the time goes:
time: 217 us; the launch traced here: 213 us
  blocking collectives  113 us (52%)
  starting transfers between devices  50.8 us (23%)
  waiting for transfers between devices  37.9 us (17%)
  matrix products  7.18 us (3%)
  local copies, waits for them, and re-layouts  3.6 us (2%)
    all_to_all x3, blocking collectives, swap(): return lax.all_to_all(blocks, axis, split_axis=0, concat_axis=0, tiled=True)  65 us
    all_gather x1, blocking collectives, local(): gathered = lax.all_gather(payload, ('far', 'mid'), axis=0)  47.6 us
    ppermute x3, starting transfers between devices, local(): lax.ppermute(away[step - 1], 'far', [(i, (i + step) % far) for i in range...  29.4 us
    all_to_all x2, waiting for transfers between devices, swap(): return lax.all_to_all(blocks, axis, split_axis=0, concat_axis=0, tiled=True)  24.6 us
    all_to_all x2, starting transfers between devices, swap(): return lax.all_to_all(blocks, axis, split_axis=0, concat_axis=0, tiled=True)  21.4 us
    ppermute x3, waiting for transfers between devices, local(): lax.ppermute(away[step - 1], 'far', [(i, (i + step) % far) for i in range...  13.3 us
  transfers between devices with their start and end apart: 5, of which 3 were waited for; matrix products, arithmetic and copies ran while one was open for 2% of the time, Pallas kernels for 0%

commit v1 on v0

--- a/solution.py
+++ b/solution.py
@@ -5,6 +5,7 @@
 
 FAR = 4
 MID = 4
+LANES = 128
 NODES = ("far", "mid", "near")
 
 
@@ -39,6 +40,23 @@
 def spread(block, axis):
     size = lax.axis_size(axis)
     return swap(jnp.broadcast_to(block[None], (size, *block.shape)), axis)
+
+
+def pack(blocks):
+    rows, features = blocks.shape[1:]
+    whole = features // LANES
+    parts = [blocks[:, :, k * LANES : (k + 1) * LANES] for k in range(whole)]
+    rest = blocks[:, :, whole * LANES :]
+    parts.append(jnp.concatenate([rest[:, : rows // 2], rest[:, rows // 2 :]], axis=2))
+    return jnp.concatenate(parts, axis=1)
+
+
+def unpack(packed, rows):
+    whole = packed.shape[1] // rows
+    parts = [packed[:, k * rows : (k + 1) * rows] for k in range(whole)]
+    rest = packed[:, whole * rows :]
+    parts.append(jnp.concatenate([rest[:, :, : LANES // 2], rest[:, :, LANES // 2 :]], axis=1))
+    return jnp.concatenate(parts, axis=2)
 
 
 def local(hidden_in, expert_ids, gate_weights, w_in, w_down):
@@ -99,7 +117,9 @@
             sum(jnp.where(hit & placed, gates[:, :, k, None], 0) for k, hit in enumerate(named))
         )
 
-    returned = swap(expert_out, ("mid", "near")).transpose(1, 0, 2, 3)
+    returned = pack(expert_out.reshape(mid * near, far * capacity, features))
+    returned = unpack(swap(returned, ("mid", "near")), far * capacity)
+    returned = returned.reshape(mid * near, far, capacity, features).transpose(1, 0, 2, 3)
     returned = returned.reshape(far, mid * near * capacity, features)
 
     def block_sums(first, last):

time: 217 us -> 215 us (level)
    all_to_all x2, waiting for transfers between devices: 24.6 us -> 22.3 us  [swap(): return lax.all_to_all(blocks, axis, split_axis=0, concat_axis=0, tiled=True)]
  transfers between devices with their start and end apart: 5 -> 5, of which waited for: 3 -> 2; matrix products, arithmetic and copies ran while one was open for 2% -> 2% of each run, Pallas kernels for 0% -> 0%
where the time goes in v1:
time: 215 us; the launch traced here: 212 us
  blocking collectives  113 us (53%)
  starting transfers between devices  50.8 us (24%)
  waiting for transfers between devices  36 us (17%)
  matrix products  7.19 us (3%)
  local copies, waits for them, and re-layouts  3.02 us (1%)
    all_to_all x3, blocking collectives, swap(): return lax.all_to_all(blocks, axis, split_axis=0, concat_axis=0, tiled=True)  65 us
    all_gather x1, blocking collectives, local(): gathered = lax.all_gather(payload, ('far', 'mid'), axis=0)  47.6 us
    ppermute x3, starting transfers between devices, local(): lax.ppermute(away[step - 1], 'far', [(i, (i + step) % far) for i in range...  29.4 us
    all_to_all x2, waiting for transfers between devices, swap(): return lax.all_to_all(blocks, axis, split_axis=0, concat_axis=0, tiled=True)  22.3 us
    all_to_all x2, starting transfers between devices, swap(): return lax.all_to_all(blocks, axis, split_axis=0, concat_axis=0, tiled=True)  21.4 us
    ppermute x3, waiting for transfers between devices, local(): lax.ppermute(away[step - 1], 'far', [(i, (i + step) % far) for i in range...  13.7 us
  transfers between devices with their start and end apart: 5, of which 2 were waited for; matrix products, arithmetic and copies ran while one was open for 2% of the time, Pallas kernels for 0%

profile of v1, /device:TPU:6, one launch (start us, length us, event | category | flops | bytes accessed | tf_op | source)
XLA Modules:
  0.0 211.9 jit_solution(10085707107541352567)
XLA Ops:
  0.0 17.5 %all-to-all-start = ((bf16[16,448,128]{2,1,0:T(8,128)(2,1)}), bf16[16,448,128]{2,1,0:T(8,128)(2,1)}, u32[]{:S(2)}, u32[]{:S(2)}) async-start(bf16[16,448,128]{2,1,0:T(8,128)(2,1)} %bitcast.114), calls=%async_computation | async-start | bytes 3670016 | tf_op jit(solution)/shard_map/all_to_all | solution.py:37
  18.1 47.6 %all-gather = bf16[1024,464]{1,0:T(8,128)(2,1)S(1)} all-gather(bf16[64,464]{1,0:T(8,128)(2,1)S(1)} %concatenate.22), channel_id=2, replica_groups=mesh['far'=4,'mid'=4,'near'=4,'local'=16] {'far','mid'}, dimensions={0}, use_global_device_ids=true | all-gather | bytes 1009664 | tf_op jit(solution)/shard_map/all_gather | solution.py:78
  65.7 0.4 fusion.6
  66.3 1.6 slice_reduce_fusion.3
  67.9 0.5 fusion
  68.5 11.2 %all_to_all.25 = bf16[4,16,8,448]{3,2,1,0:T(8,128)(2,1)S(1)} all-to-all(bf16[4,16,8,448]{3,2,1,0:T(8,128)(2,1)S(1)} %bitcast.112), channel_id=1, replica_groups=mesh['far'=4,'mid'=4,'near'=4,'local'=16] {'near'}, dimensions={0} | all-to-all | bytes 917504 | tf_op jit(solution)/shard_map/all_to_all | solution.py:37
  79.8 2.8 %convert_bitcast_fusion = bf16[16,512,128]{1,2,0:T(8,128)(2,1)S(1)} fusion(bf16[16,448,128]{2,1,0:T(8,128)(2,1)} %all-to-all-done, bf16[512,448,1]{1,0,2:T(8,128)(2,1)S(1)} %bitcast.116), kind=kOutput, calls=%fused_computation.3 | convolution fusion | flops 940572672 | bytes 4390912 | tf_op jit(solution)/shard_map/rd,ldj->lrj/dot_general | solution.py:95
  82.6 34.6 %all_to_all.26 = bf16[16,512,128]{1,2,0:T(8,128)(2,1)S(1)} all-to-all(bf16[16,512,128]{1,2,0:T(8,128)(2,1)S(1)} %convert_bitcast_fusion), channel_id=1, replica_groups=mesh['far'=4,'mid'=4,'near'=4,'local'=16] {'local'}, dimensions={0} | all-to-all | bytes 4194304 | tf_op jit(solution)/shard_map/all_to_all | solution.py:37
  117.3 0.3 convert_reduce_fusion
  117.7 19.1 %all_to_all.27 = bf16[16,64,512]{2,1,0:T(8,128)(2,1)S(1)} all-to-all(bf16[16,64,512]{2,1,0:T(8,128)(2,1)S(1)} %broadcast_in_dim.131), channel_id=1, replica_groups=mesh['far'=4,'mid'=4,'near'=4,'local'=16] {'local'}, dimensions={0} | all-to-all | bytes 2097152 | tf_op jit(solution)/shard_map/all_to_all | solution.py:37
  136.8 0.6 convolution_convert_fusion.1
  137.5 0.2 copy.48
  137.8 0.9 maximum_maximum_fusion
  138.7 3.9 %all-to-all-start.4 = ((bf16[16,112,128]{2,1,0:T(8,128)(2,1)}), bf16[16,112,128]{2,1,0:T(8,128)(2,1)S(1)}, u32[]{:S(2)}, u32[]{:S(2)}) async-start(bf16[16,112,128]{2,1,0:T(8,128)(2,1)} %maximum_maximum_fusion), calls=%async_computation.4 | async-start | bytes 917504 | tf_op jit(solution)/shard_map/all_to_all | solution.py:37
  142.9 0.9 select_add_fusion
  143.8 22.3 %all-to-all-done.4 = bf16[16,112,128]{2,1,0:T(8,128)(2,1)S(1)} async-done(((bf16[16,112,128]{2,1,0:T(8,128)(2,1)}), bf16[16,112,128]{2,1,0:T(8,128)(2,1)S(1)}, u32[]{:S(2)}, u32[]{:S(2)}) %all-to-all-start.4) | async-done | bytes 458784 | tf_op jit(solution)/shard_map/all_to_all | solution.py:37
  166.5 0.4 fusion.11
  166.9 0.4 convolution_add_fusion.1
  167.3 0.4 fusion.1
  167.7 14.9 %collective-permute-start = (bf16[64,448]{1,0:T(8,128)(2,1)S(1)}, bf16[64,448]{1,0:T(8,128)(2,1)S(1)}, u32[]{:S(2)}, u32[]{:S(2)}) collective-permute-start(bf16[64,448]{1,0:T(8,128)(2,1)S(1)} %get-tuple-element.23), channel_id=1, source_target_pairs={{0,512},{256,768},{512,0},{768,256},{1,513},{257,769},{513,1},{769... | collective-permute-start | bytes 172040 | tf_op jit(solution)/shard_map/ppermute | solution.py:138
  182.6 6.3 %collective-permute-start.2 = (bf16[64,448]{1,0:T(8,128)(2,1)S(1)}, bf16[64,448]{1,0:T(8,128)(2,1)S(1)}, u32[]{:S(2)}, u32[]{:S(2)}) collective-permute-start(bf16[64,448]{1,0:T(8,128)(2,1)S(1)} %get-tuple-element.24), channel_id=1, source_target_pairs={{0,768},{256,0},{512,256},{768,512},{1,769},{257,1},{513,257},{769... | collective-permute-start | bytes 172040 | tf_op jit(solution)/shard_map/ppermute | solution.py:138
  188.9 8.3 %collective-permute-start.1 = (bf16[64,448]{1,0:T(8,128)(2,1)S(1)}, bf16[64,448]{1,0:T(8,128)(2,1)S(1)}, u32[]{:S(2)}, u32[]{:S(2)}) collective-permute-start(bf16[64,448]{1,0:T(8,128)(2,1)S(1)} %get-tuple-element.25), channel_id=1, source_target_pairs={{0,256},{256,512},{512,768},{768,0},{1,257},{257,513},{513,769},{7... | collective-permute-start | bytes 172040 | tf_op jit(solution)/shard_map/ppermute | solution.py:138
  197.4 13.7 %collective-permute-done.2 = bf16[64,448]{1,0:T(8,128)(2,1)S(1)} collective-permute-done((bf16[64,448]{1,0:T(8,128)(2,1)S(1)}, bf16[64,448]{1,0:T(8,128)(2,1)S(1)}, u32[]{:S(2)}, u32[]{:S(2)}) %collective-permute-start.2) | collective-permute-done | bytes 57376 | tf_op jit(solution)/shard_map/ppermute | solution.py:138
  211.1 0.8 add_convert_fusion
  (39 shorter events, 1.9 us)
Async XLA Ops:
  0.0 136.8 %copy-start = (bf16[1,1024,448]{1,2,0:T(8,128)(2,1)S(1)}, bf16[1,1024,448]{1,2,0:T(8,128)(2,1)}, u32[]{:S(2)}) copy-start(bf16[1,1024,448]{1,2,0:T(8,128)(2,1)} %param.9) | copy-start | bytes 2752516
  0.0 17.5 %copy-start.3 = (f32[64,4]{0,1:T(4,128)S(1)}, f32[64,4]{0,1:T(4,128)}, u32[]{:S(2)}) copy-start(f32[64,4]{0,1:T(4,128)} %param.7) | copy-start | bytes 3076
  0.0 17.6 %copy-start.2 = (s32[64,4]{0,1:T(4,128)S(1)}, s32[64,4]{0,1:T(4,128)}, u32[]{:S(2)}) copy-start(s32[64,4]{0,1:T(4,128)} %param.6) | copy-start | bytes 3076
  0.0 18.0 %copy-start.1 = (bf16[64,448]{1,0:T(8,128)(2,1)S(1)}, bf16[64,448]{1,0:T(8,128)(2,1)}, u32[]{:S(2)}) copy-start(bf16[64,448]{1,0:T(8,128)(2,1)} %param.5) | copy-start | bytes 172036
  0.0 68.4 %all-to-all-start = ((bf16[16,448,128]{2,1,0:T(8,128)(2,1)}), bf16[16,448,128]{2,1,0:T(8,128)(2,1)}, u32[]{:S(2)}, u32[]{:S(2)}) async-start(bf16[16,448,128]{2,1,0:T(8,128)(2,1)} %bitcast.114), calls=%async_computation | async-start | bytes 3670016 | tf_op jit(solution)/shard_map/all_to_all | solution.py:37
  138.7 27.4 %all-to-all-start.4 = ((bf16[16,112,128]{2,1,0:T(8,128)(2,1)}), bf16[16,112,128]{2,1,0:T(8,128)(2,1)S(1)}, u32[]{:S(2)}, u32[]{:S(2)}) async-start(bf16[16,112,128]{2,1,0:T(8,128)(2,1)} %maximum_maximum_fusion), calls=%async_computation.4 | async-start | bytes 917504 | tf_op jit(solution)/shard_map/all_to_all | solution.py:37
  167.7 29.6 %collective-permute-start = (bf16[64,448]{1,0:T(8,128)(2,1)S(1)}, bf16[64,448]{1,0:T(8,128)(2,1)S(1)}, u32[]{:S(2)}, u32[]{:S(2)}) collective-permute-start(bf16[64,448]{1,0:T(8,128)(2,1)S(1)} %get-tuple-element.23), channel_id=1, source_target_pairs={{0,512},{256,768},{512,0},{768,256},{1,513},{257,769},{513,1},{769... | collective-permute-start | bytes 172040 | tf_op jit(solution)/shard_map/ppermute | solution.py:138
  182.6 28.4 %collective-permute-start.2 = (bf16[64,448]{1,0:T(8,128)(2,1)S(1)}, bf16[64,448]{1,0:T(8,128)(2,1)S(1)}, u32[]{:S(2)}, u32[]{:S(2)}) collective-permute-start(bf16[64,448]{1,0:T(8,128)(2,1)S(1)} %get-tuple-element.24), channel_id=1, source_target_pairs={{0,768},{256,0},{512,256},{768,512},{1,769},{257,1},{513,257},{769... | collective-permute-start | bytes 172040 | tf_op jit(solution)/shard_map/ppermute | solution.py:138
  188.9 22.2 %collective-permute-start.1 = (bf16[64,448]{1,0:T(8,128)(2,1)S(1)}, bf16[64,448]{1,0:T(8,128)(2,1)S(1)}, u32[]{:S(2)}, u32[]{:S(2)}) collective-permute-start(bf16[64,448]{1,0:T(8,128)(2,1)S(1)} %get-tuple-element.25), channel_id=1, source_target_pairs={{0,256},{256,512},{512,768},{768,0},{1,257},{257,513},{513,769},{7... | collective-permute-start | bytes 172040 | tf_op jit(solution)/shard_map/ppermute | solution.py:138

commit v2 on v1

--- a/solution.py
+++ b/solution.py
@@ -133,14 +133,14 @@
             for piece in combine
         )
 
-    away = block_sums(1, far).astype(jnp.bfloat16)
+    away = pack(block_sums(1, far).astype(jnp.bfloat16))
     sent = [
         lax.ppermute(away[step - 1], "far", [(i, (i + step) % far) for i in range(far)])
         for step in sorted(range(1, far), key=lambda step: -min(step, far - step))
     ]
     mixed = block_sums(0, 1)[0]
     for block in sent:
-        mixed += block.astype(jnp.float32)
+        mixed += unpack(block[None], tok_count)[0].astype(jnp.float32)
     return mixed.astype(jnp.bfloat16)
 
 

time: 215 us -> 216 us (level)
  the two profiles are of different devices: /device:TPU:6 before, /device:TPU:192 now
where the time goes in v2:
time: 216 us; the launch traced here: 215 us
  blocking collectives  115 us (53%)
  starting transfers between devices  47.4 us (22%)
  waiting for transfers between devices  39.8 us (18%)
  matrix products  7.18 us (3%)
  local copies, waits for them, and re-layouts  3.29 us (2%)
    all_to_all x3, blocking collectives, swap(): return lax.all_to_all(blocks, axis, split_axis=0, concat_axis=0, tiled=True)  66.6 us
    all_gather x1, blocking collectives, local(): gathered = lax.all_gather(payload, ('far', 'mid'), axis=0)  48.9 us
    ppermute x3, starting transfers between devices, local(): lax.ppermute(away[step - 1], 'far', [(i, (i + step) % far) for i in range...  29.4 us
    ppermute x3, waiting for transfers between devices, local(): lax.ppermute(away[step - 1], 'far', [(i, (i + step) % far) for i in range...  21 us
    all_to_all x2, waiting for transfers between devices, swap(): return lax.all_to_all(blocks, axis, split_axis=0, concat_axis=0, tiled=True)  18.8 us
    all_to_all x2, starting transfers between devices, swap(): return lax.all_to_all(blocks, axis, split_axis=0, concat_axis=0, tiled=True)  18 us
  transfers between devices with their start and end apart: 5, of which 2 were waited for; matrix products, arithmetic and copies ran while one was open for 2% of the time, Pallas kernels for 0%

profile of v2, /device:TPU:192, one launch (start us, length us, event | category | flops | bytes accessed | tf_op | source)
XLA Modules:
  0.0 215.4 jit_solution(1512041078169737773)
XLA Ops:
  0.0 7.2 %all-to-all-start = ((bf16[16,448,128]{2,1,0:T(8,128)(2,1)}), bf16[16,448,128]{2,1,0:T(8,128)(2,1)}, u32[]{:S(2)}, u32[]{:S(2)}) async-start(bf16[16,448,128]{2,1,0:T(8,128)(2,1)} %bitcast.130), calls=%async_computation | async-start | bytes 3670016 | tf_op jit(solution)/shard_map/all_to_all | solution.py:37
  7.9 48.9 %all-gather = bf16[1024,464]{1,0:T(8,128)(2,1)S(1)} all-gather(bf16[64,464]{1,0:T(8,128)(2,1)S(1)} %concatenate.46), channel_id=2, replica_groups=mesh['far'=4,'mid'=4,'near'=4,'local'=16] {'far','mid'}, dimensions={0}, use_global_device_ids=true | all-gather | bytes 1009664 | tf_op jit(solution)/shard_map/all_gather | solution.py:78
  56.8 0.4 fusion.10
  57.4 1.6 slice_reduce_fusion.3
  58.9 0.5 fusion
  59.5 13.0 %all_to_all.25 = bf16[4,16,8,448]{3,2,1,0:T(8,128)(2,1)S(1)} all-to-all(bf16[4,16,8,448]{3,2,1,0:T(8,128)(2,1)S(1)} %bitcast.128), channel_id=1, replica_groups=mesh['far'=4,'mid'=4,'near'=4,'local'=16] {'near'}, dimensions={0} | all-to-all | bytes 917504 | tf_op jit(solution)/shard_map/all_to_all | solution.py:37
  72.6 2.8 %convert_bitcast_fusion = bf16[16,512,128]{1,2,0:T(8,128)(2,1)S(1)} fusion(bf16[16,448,128]{2,1,0:T(8,128)(2,1)} %all-to-all-done, bf16[512,448,1]{1,0,2:T(8,128)(2,1)S(1)} %bitcast.132), kind=kOutput, calls=%fused_computation.3 | convolution fusion | flops 940572672 | bytes 4390912 | tf_op jit(solution)/shard_map/rd,ldj->lrj/dot_general | solution.py:95
  75.4 34.5 %all_to_all.26 = bf16[16,512,128]{1,2,0:T(8,128)(2,1)S(1)} all-to-all(bf16[16,512,128]{1,2,0:T(8,128)(2,1)S(1)} %convert_bitcast_fusion), channel_id=1, replica_groups=mesh['far'=4,'mid'=4,'near'=4,'local'=16] {'local'}, dimensions={0} | all-to-all | bytes 4194304 | tf_op jit(solution)/shard_map/all_to_all | solution.py:37
  109.9 0.3 convert_reduce_fusion
  110.3 19.1 %all_to_all.27 = bf16[16,64,512]{2,1,0:T(8,128)(2,1)S(1)} all-to-all(bf16[16,64,512]{2,1,0:T(8,128)(2,1)S(1)} %broadcast_in_dim.140), channel_id=1, replica_groups=mesh['far'=4,'mid'=4,'near'=4,'local'=16] {'local'}, dimensions={0} | all-to-all | bytes 2097152 | tf_op jit(solution)/shard_map/all_to_all | solution.py:37
  129.4 0.6 convolution_convert_fusion.1
  130.1 0.2 copy.48
  130.4 0.9 maximum_maximum_fusion
  131.3 10.7 %all-to-all-start.4 = ((bf16[16,112,128]{2,1,0:T(8,128)(2,1)}), bf16[16,112,128]{2,1,0:T(8,128)(2,1)S(1)}, u32[]{:S(2)}, u32[]{:S(2)}) async-start(bf16[16,112,128]{2,1,0:T(8,128)(2,1)} %maximum_maximum_fusion), calls=%async_computation.4 | async-start | bytes 917504 | tf_op jit(solution)/shard_map/all_to_all | solution.py:37
  142.3 0.9 select_add_fusion
  143.2 18.8 %all-to-all-done.4 = bf16[16,112,128]{2,1,0:T(8,128)(2,1)S(1)} async-done(((bf16[16,112,128]{2,1,0:T(8,128)(2,1)}), bf16[16,112,128]{2,1,0:T(8,128)(2,1)S(1)}, u32[]{:S(2)}, u32[]{:S(2)}) %all-to-all-start.4) | async-done | bytes 458784 | tf_op jit(solution)/shard_map/all_to_all | solution.py:37
  162.2 0.4 fusion.15
  162.6 0.4 convolution_add_fusion.1
  163.1 0.4 fusion.1
  163.8 9.4 %collective-permute-start.2 = (bf16[224,128]{1,0:T(8,128)(2,1)S(1)}, bf16[224,128]{1,0:T(8,128)(2,1)S(1)}, u32[]{:S(2)}, u32[]{:S(2)}) collective-permute-start(bf16[224,128]{1,0:T(8,128)(2,1)S(1)} %get-tuple-element.28), channel_id=1, source_target_pairs={{0,768},{256,0},{512,256},{768,512},{1,769},{257,1},{513,257},{769... | collective-permute-start | bytes 172040 | tf_op jit(solution)/shard_map/ppermute | solution.py:138
  173.2 5.2 %collective-permute-start.1 = (bf16[224,128]{1,0:T(8,128)(2,1)S(1)}, bf16[224,128]{1,0:T(8,128)(2,1)S(1)}, u32[]{:S(2)}, u32[]{:S(2)}) collective-permute-start(bf16[224,128]{1,0:T(8,128)(2,1)S(1)} %get-tuple-element.29), channel_id=1, source_target_pairs={{0,256},{256,512},{512,768},{768,0},{1,257},{257,513},{513,769},{7... | collective-permute-start | bytes 172040 | tf_op jit(solution)/shard_map/ppermute | solution.py:138
  178.4 14.9 %collective-permute-start = (bf16[224,128]{1,0:T(8,128)(2,1)S(1)}, bf16[224,128]{1,0:T(8,128)(2,1)S(1)}, u32[]{:S(2)}, u32[]{:S(2)}) collective-permute-start(bf16[224,128]{1,0:T(8,128)(2,1)S(1)} %get-tuple-element.30), channel_id=1, source_target_pairs={{0,512},{256,768},{512,0},{768,256},{1,513},{257,769},{513,1},{769... | collective-permute-start | bytes 172040 | tf_op jit(solution)/shard_map/ppermute | solution.py:138
  193.6 21.0 %collective-permute-done = bf16[224,128]{1,0:T(8,128)(2,1)S(1)} collective-permute-done((bf16[224,128]{1,0:T(8,128)(2,1)S(1)}, bf16[224,128]{1,0:T(8,128)(2,1)S(1)}, u32[]{:S(2)}, u32[]{:S(2)}) %collective-permute-start) | collective-permute-done | bytes 57376 | tf_op jit(solution)/shard_map/ppermute | solution.py:138
  214.6 0.8 fusion.5
  (48 shorter events, 2.2 us)
Async XLA Ops:
  0.0 129.4 %copy-start = (bf16[1,1024,448]{1,2,0:T(8,128)(2,1)S(1)}, bf16[1,1024,448]{1,2,0:T(8,128)(2,1)}, u32[]{:S(2)}) copy-start(bf16[1,1024,448]{1,2,0:T(8,128)(2,1)} %param.9) | copy-start | bytes 2752516
  0.0 7.3 %copy-start.3 = (f32[64,4]{0,1:T(4,128)S(1)}, f32[64,4]{0,1:T(4,128)}, u32[]{:S(2)}) copy-start(f32[64,4]{0,1:T(4,128)} %param.7) | copy-start | bytes 3076
  0.0 7.4 %copy-start.2 = (s32[64,4]{0,1:T(4,128)S(1)}, s32[64,4]{0,1:T(4,128)}, u32[]{:S(2)}) copy-start(s32[64,4]{0,1:T(4,128)} %param.6) | copy-start | bytes 3076
  0.0 7.8 %copy-start.1 = (bf16[64,448]{1,0:T(8,128)(2,1)S(1)}, bf16[64,448]{1,0:T(8,128)(2,1)}, u32[]{:S(2)}) copy-start(bf16[64,448]{1,0:T(8,128)(2,1)} %param.5) | copy-start | bytes 172036
  0.0 59.5 %all-to-all-start = ((bf16[16,448,128]{2,1,0:T(8,128)(2,1)}), bf16[16,448,128]{2,1,0:T(8,128)(2,1)}, u32[]{:S(2)}, u32[]{:S(2)}) async-start(bf16[16,448,128]{2,1,0:T(8,128)(2,1)} %bitcast.130), calls=%async_computation | async-start | bytes 3670016 | tf_op jit(solution)/shard_map/all_to_all | solution.py:37
  131.3 30.8 %all-to-all-start.4 = ((bf16[16,112,128]{2,1,0:T(8,128)(2,1)}), bf16[16,112,128]{2,1,0:T(8,128)(2,1)S(1)}, u32[]{:S(2)}, u32[]{:S(2)}) async-start(bf16[16,112,128]{2,1,0:T(8,128)(2,1)} %maximum_maximum_fusion), calls=%async_computation.4 | async-start | bytes 917504 | tf_op jit(solution)/shard_map/all_to_all | solution.py:37
  163.8 29.6 %collective-permute-start.2 = (bf16[224,128]{1,0:T(8,128)(2,1)S(1)}, bf16[224,128]{1,0:T(8,128)(2,1)S(1)}, u32[]{:S(2)}, u32[]{:S(2)}) collective-permute-start(bf16[224,128]{1,0:T(8,128)(2,1)S(1)} %get-tuple-element.28), channel_id=1, source_target_pairs={{0,768},{256,0},{512,256},{768,512},{1,769},{257,1},{513,257},{769... | collective-permute-start | bytes 172040 | tf_op jit(solution)/shard_map/ppermute | solution.py:138
  173.2 20.3 %collective-permute-start.1 = (bf16[224,128]{1,0:T(8,128)(2,1)S(1)}, bf16[224,128]{1,0:T(8,128)(2,1)S(1)}, u32[]{:S(2)}, u32[]{:S(2)}) collective-permute-start(bf16[224,128]{1,0:T(8,128)(2,1)S(1)} %get-tuple-element.29), channel_id=1, source_target_pairs={{0,256},{256,512},{512,768},{768,0},{1,257},{257,513},{513,769},{7... | collective-permute-start | bytes 172040 | tf_op jit(solution)/shard_map/ppermute | solution.py:138
  178.4 36.2 %collective-permute-start = (bf16[224,128]{1,0:T(8,128)(2,1)S(1)}, bf16[224,128]{1,0:T(8,128)(2,1)S(1)}, u32[]{:S(2)}, u32[]{:S(2)}) collective-permute-start(bf16[224,128]{1,0:T(8,128)(2,1)S(1)} %get-tuple-element.30), channel_id=1, source_target_pairs={{0,512},{256,768},{512,0},{768,256},{1,513},{257,769},{513,1},{769... | collective-permute-start | bytes 172040 | tf_op jit(solution)/shard_map/ppermute | solution.py:138
